TPU v7x, 32 devices: a whole 2x2x4 slice. The times are simulated.
32 devices in a mesh: ctx: 16 (over z, y, x), head: 2 (over core).
Axes of the slice: x: 2, y: 2, z: 4, core: 2. Of those that a mesh axis runs over, the one named last changes fastest.
Arguments:
- queries: bfloat16 [2048, 4096], P('ctx', 'head'), may hold values from -45 to 45
- kv_rows: bfloat16 [2048, 512], P('ctx'), may hold values from -6 to 6
- doc_start: int32 [64], replicated, may hold values from 0 to 2016, as said below
- destination: int32 [64], replicated, may hold values from 0 to 63, as said below
- out_weight: bfloat16 [4096, 2048], P('head'), may hold values from -0.5 to 0.5
Outputs:
- mixed: bfloat16 [2048, 2048], P('head', 'ctx')
Inputs may be any that keep to these rules, and one draw needn't show every extreme that they name: Documents are runs of whole blocks: doc_start[b] is a multiple of 32, at most b * 32, never falls from block to block, and equals b * 32 where a document begins; doc_start[0] = 0. `destination`: A permutation of 0 .. 63 that maps every aligned group of 16 consecutive blocks onto itself.
All inputs are finite; a program needn't handle non-finite values.
Results may differ from a plain program's by a relative error of at most 0.011.
Values may be sent and summed in bfloat16 or wider, within the bound.
No kernel may reach another device: no remote copies, remote signals or barrier semaphores. Data moves between devices by JAX's collectives and lax.ppermute only.
A program may use at most 64 MiB of HBM per device.

v0:
```python
import functools

import jax
import jax.numpy as jnp
import numpy as np
from jax import lax
from jax.experimental import pallas as pl
from jax.experimental.pallas import tpu as pltpu
from jax.sharding import PartitionSpec as P

DH = 128
W1 = 512
W2 = 32
QB = 32
LANES = 128
PACK = 16
VR = DH + PACK
SAMPLE = 32
AHEAD = 3
SPAN = 4
LIMIT = 1e30
LOG2E = 1.4426950408889634


def iota(shape, dim):
    return lax.broadcasted_iota(jnp.int32, shape, dim)


def spread(columns, first, heads):
    pick = iota((columns.shape[1], LANES), 0) == first + iota((columns.shape[1], LANES), 1) // heads
    pick = pick.astype(jnp.float32).astype(jnp.bfloat16)
    return jnp.dot(columns, pick, preferred_element_type=jnp.float32)


def with_ones(values):
    return jnp.concatenate(
        [values.astype(jnp.float32).T, jnp.ones((VR - DH, LANES), jnp.float32)], axis=0
    ).astype(jnp.bfloat16)


GROUP = 4


def plan_places(blocks):
    room = blocks // 2
    sizes = (blocks, 1, blocks, GROUP - 1, blocks + (GROUP - 1) * room, GROUP * blocks, 1)
    return [sum(sizes[:k]) for k in range(len(sizes) + 1)]


def make_plan(table_ref, plan_ref, blocks):
    room = blocks // 2
    position, here = table_ref[0], table_ref[1]
    total = (table_ref.shape[0] - 2) // 2
    target = 2 + total
    place = lax.rem(position, GROUP)
    masked, head, order, sent, some, whole, _, _ = plan_places(blocks)
    one, zero = jnp.int32(1), jnp.int32(0)
    for k in range(blocks):
        block = position * blocks + k
        outside = table_ref[2 + block] - (block * QB - W1)
        plan_ref[masked + k] = jnp.clip(outside, 0, W1)
    plan_ref[head] = here
    for r in range(GROUP):
        source = lax.bitwise_xor(place, jnp.int32(r))
        slots = [table_ref[target + (position - place + source) * blocks + k] for k in range(blocks)]
        far = [lax.bitwise_xor(lax.rem(lax.div(s, blocks), GROUP), source) for s in slots]
        for k in range(blocks):
            at = zero
            for j in range(blocks):
                if j != k:
                    ahead = far[j] <= far[k] if j < k else far[j] < far[k]
                    at = at + jnp.where(ahead, one, zero)
            plan_ref[whole + r * blocks + at] = slots[k]
            if r == 0:
                plan_ref[order + k] = at
        for distance in range(1, GROUP) if r == 0 else (r,):
            nearer = zero
            for k in range(blocks):
                nearer = nearer + jnp.where(far[k] < distance, one, zero)
            nearer = jnp.minimum(nearer, blocks - room)
            if r == 0:
                plan_ref[sent + distance - 1] = nearer
            else:
                for c in range(room):
                    into = some + blocks + (r - 1) * room + c
                    plan_ref[into] = plan_ref[whole + r * blocks + nearer + c]
    for k in range(blocks):
        plan_ref[some + k] = plan_ref[whole + k]


def own_kernel(q_ref, kv_ref, q3, k1o, v1o, k2o, v2o):
    f32, bf16 = jnp.float32, jnp.bfloat16
    tokens = q_ref.shape[0]
    heads = q_ref.shape[1] // DH
    group = LANES // heads
    k1o[...] = kv_ref[:, :DH]
    second = kv_ref[:, 2 * DH : 3 * DH].astype(f32)
    second = jnp.broadcast_to(second[:, None, :], (tokens, heads, DH))
    k2o[...] = second.reshape(k2o.shape).astype(bf16)
    for k in range(tokens // LANES):
        v1o[k] = with_ones(kv_ref[k * LANES : (k + 1) * LANES, DH : 2 * DH])
        columns = with_ones(kv_ref[k * LANES : (k + 1) * LANES, 3 * DH :])
        for c in range(heads):
            v2o[k * heads + c] = spread(columns, c * group, heads)
    for h in range(heads):
        q3[pl.ds(h, tokens, stride=heads), :] = q_ref[:, h * DH : (h + 1) * DH].astype(f32)


def attention_kernel(pairs, outputs, table_ref, q3, k1o, v1o, k2o, v2o, w_ref, *refs):
    shards, refs = refs[:pairs], refs[pairs:]
    out_refs, plan_ref, pick_ref, refs = refs[:outputs], refs[outputs], refs[outputs + 1], refs[outputs + 2 :]
    kv_ref, wbuf, wsem, k1n, k1s, v1t, v1n, k2x, v2x, rowid, laneid, part, top2, bad, rows = refs
    tokens = k1o.shape[0]
    heads = q3.shape[0] // tokens
    cols = W2 * heads
    group = LANES // heads
    tiles = tokens // LANES
    blocks = tokens // QB
    near_tiles = cols // LANES
    size = max(heads, PACK)
    pack = size // heads
    wide = min(2 * LANES, cols)
    span = min(SPAN, QB // group)
    scale = LOG2E / np.sqrt(DH)
    f32, bf16 = jnp.float32, jnp.bfloat16

    room = blocks // 2
    total = (table_ref.shape[0] - 2) // 2
    senders = total // blocks

    def most_alike(device):
        to = [lax.rem(lax.div(table_ref[2 + total + device * blocks + k], blocks), GROUP) for k in range(blocks)]
        most = jnp.int32(1)
        for k in range(blocks - room):
            alike = jnp.int32(1)
            for j in range(k + 1, blocks):
                alike = alike + jnp.where(to[j] == to[k], 1, 0).astype(jnp.int32)
            most = jnp.maximum(most, alike)
        return most

    def either(cond, a, b):
        if isinstance(cond, bool):
            return a if cond else b
        return jnp.where(cond, a, b)

    weight_copy = pltpu.make_async_copy(w_ref, wbuf, wsem)
    weight_copy.start()
    masked, head, order, sent, _, _, small, _ = plan_places(blocks)
    here = table_ref[1]
    make_plan(table_ref, plan_ref, blocks)

    def lay(order):
        at = 0
        for ref in order:
            kv_ref[at : at + ref.shape[0], :] = ref[...]
            at += ref.shape[0]

    if outputs == 2:

        @pl.when(here == 0)
        def _():
            lay(shards[::-1])

        @pl.when(here != 0)
        def _():
            lay(shards)

    else:
        lay(shards)

    def prepare():
        rowid[...] = iota(rowid.shape, 0).astype(f32).astype(bf16)
        laneid[...] = iota(laneid.shape, 1).astype(f32).astype(bf16)
        bad[...] = jnp.zeros_like(bad)
        k1n[...] = k1o[...]
        v1n[...] = v1o[...]
        second = kv_ref[W1 - W2 :, 2 * DH : 3 * DH].astype(f32)
        second = jnp.broadcast_to(second[:, None, :], (W2, heads, DH))
        k2x[: W2 // pack] = second.reshape(W2 // pack, size, DH).astype(bf16)
        k2x[W2 // pack :] = k2o[...]
        columns = with_ones(kv_ref[W1 - LANES :, 3 * DH :])
        for k in range(near_tiles):
            v2x[k] = spread(columns, LANES - W2 + k * group, heads)
        v2x[near_tiles:] = v2o[...]

    def reset(t, inv):
        kt = k1o[pl.ds(pl.multiple_of(t, PACK), PACK), :].astype(f32)[:1]
        window = kv_ref[:, : 2 * DH].astype(f32)
        ok = iota((W1, DH), 0) >= inv
        k1s[...] = jnp.where(ok, window[:, :DH], kt).astype(bf16)
        values = jnp.where(ok, window[:, DH:], 0.0)
        for k in range(W1 // LANES):
            v1t[k, :DH] = values[k * LANES : (k + 1) * LANES].T.astype(bf16)
            live = k * LANES + iota((VR - DH, LANES), 1) >= inv
            v1t[k, DH:] = live.astype(f32).astype(bf16)
        k1n[...] = jnp.where(iota((tokens, DH), 0) < t, kt, k1n[...].astype(f32)).astype(bf16)
        for k in range(tiles):
            gone = k * LANES + iota((VR, LANES), 1) < t
            v1n[k] = jnp.where(gone, 0.0, v1n[k].astype(f32)).astype(bf16)

        @pl.when(inv == W1)
        def _():
            fill = jnp.broadcast_to(k2x[(t + W2) // pack].astype(f32)[:1], (size, DH)).astype(bf16)
            for s in range(W2 // pack):
                k2x[t // pack + s] = fill
            for k in range(near_tiles):
                v2x[t // group + k] = jnp.zeros((VR, LANES), f32)

    def scores(g, u):
        t = g * group + u
        mark = t.astype(f32).astype(bf16)
        keys = [
            jnp.where(rowid[...] + (k * LANES) <= mark, k1n[k * LANES : (k + 1) * LANES], k1s[k * LANES : (k + 1) * LANES])
            for k in range(tiles)
        ]
        keys = jnp.concatenate(keys + [k1s[tokens:]], axis=0)
        query = q3[pl.ds(t * heads, heads), :]
        if heads < PACK:
            query = jnp.concatenate([query] * pack, axis=0)
        query = query.astype(bf16)
        base = g * (group // pack)
        for n in range(0, cols, wide):
            paired = []
            for s in range(n // size, (n + wide) // size):
                if s * pack >= group:
                    near_keys = k2x[base + s]
                elif pack == 1:
                    near_keys = k2x[base + either(s <= u, s + W2, s)]
                else:
                    token = s * pack + iota((size, DH), 0) // heads
                    after = k2x[base + s + W2 // pack].astype(f32)
                    near_keys = jnp.where(token <= u, after, k2x[base + s].astype(f32)).astype(bf16)
                paired.append(near_keys * query)
            yield lax.dot_general(
                keys,
                jnp.concatenate(paired, axis=0),
                (((1,), (1,)), ((), ())),
                preferred_element_type=f32,
            )

    def highest(logits, best=None):
        top = jnp.max(logits, axis=0, keepdims=True)
        for k in range(0, wide, LANES):
            some = top[:, k : k + LANES]
            best = some if best is None else jnp.maximum(best, some)
        return best

    def mix(g, u, n, logits, top):
        mark = (g * group + u).astype(f32).astype(bf16)
        values = [
            jnp.where(laneid[...] + (k * LANES) <= mark, v1n[k], v1t[k]) for k in range(tiles)
        ] + [v1t[k] for k in range(tiles, W1 // LANES)]
        tops = jnp.concatenate([top] * (wide // LANES), axis=1)
        product = None
        for k in range(0, W1, 2 * LANES):
            weights = jnp.exp2(logits[k : k + 2 * LANES] * scale - tops).astype(bf16)
            two = jnp.concatenate(values[k // LANES : k // LANES + 2], axis=1)
            some = jnp.dot(two, weights, preferred_element_type=f32)
            product = some if product is None else product + some
        total = None
        for c in range(0, wide, LANES):
            k = (n + c) // LANES
            near = v2x[g + k]
            if k == 0:
                near = jnp.where(iota((VR, LANES), 1) // heads <= u, v2x[g + near_tiles], near)
            some = product[:, c : c + LANES] * near
            total = some if total is None else total + some
        return total

    def keep(g, u, total, top):
        part[g * group + u] = total
        top2[g * group + u] = jnp.broadcast_to(top, (8, LANES))
        bad[...] = jnp.where(total[DH : DH + 8] < LIMIT, bad[...], 1.0)

    def finish(g):
        lane = iota((VR, LANES), 1)
        sums = []
        for u in range(group):
            top = top2[g * group + u]
            best = top
            shift = LANES // 2
            while shift >= heads:
                best = jnp.maximum(best, pltpu.roll(best, shift, 1))
                shift //= 2
            sums.append(part[g * group + u] * jnp.exp2(top - best)[:1])
        shift = heads
        while shift < LANES:
            low = lane % (2 * shift) < shift
            sums = [
                jnp.where(low, a, b) + pltpu.roll(jnp.where(low, b, a), shift, 1)
                for a, b in zip(sums[::2], sums[1::2])
            ]
            shift *= 2
        value = sums[0][:DH] * (1.0 / sums[0][DH : DH + 1])
        spot = (plan_ref[order + g * group // QB] * QB + g * group % QB) * heads
        rows[pl.ds(pl.multiple_of(spot, LANES), LANES), :] = value.T

    def run(exact):
        prepare()

        def block(b, _):
            inv = plan_ref[masked + b]
            g0 = b * (QB // group)

            @pl.when((b == 0) | (inv == W1))
            def _():
                reset(b * QB, inv)

            def fast(s, _):
                if span == QB // group:
                    each = -(-senders // blocks)
                    for k in range(each):
                        device = jnp.minimum(b * each + k, senders - 1)
                        plan_ref[small] = jnp.where(most_alike(device) > room, 0, plan_ref[small])
                work = []
                for u in range(span * group):
                    work += [(u, n) for n in range(0, cols, wide)]
                at = [divmod(u, group) for u in range(span * group)]
                first = g0 + s * span
                source = [scores(first + k, u) for k, u in at]
                top = total = None
                ahead = [next(source[u]) for u, n in work[:AHEAD]]
                for i, (u, n) in enumerate(work):
                    if i + AHEAD < len(work):
                        ahead.append(next(source[work[i + AHEAD][0]]))
                    logits = ahead.pop(0)
                    g, v = first + at[u][0], at[u][1]
                    if n == 0:
                        top = highest(logits[:SAMPLE]) * scale
                        total = None
                    some = mix(g, v, n, logits, top)
                    total = some if total is None else total + some
                    if n + wide == cols:
                        keep(g, v, total, top)
                        if v == group // 2:
                            finish(jnp.maximum(g - 1, 0))
                return 0

            def slow(s, _):
                g, u = g0 + s // group, s % group
                best = None
                for logits in scores(g, u):
                    best = highest(logits, best)
                total = None
                for n, logits in zip(range(0, cols, wide), scores(g, u)):
                    some = mix(g, u, n, logits, best * scale)
                    total = some if total is None else total + some
                keep(g, u, total, best * scale)
                return 0

            if exact:
                return lax.fori_loop(0, QB, slow, 0)
            return lax.fori_loop(0, QB // group // span, fast, 0)

        lax.fori_loop(0, tokens // QB, block, 0)
        if exact:
            lax.fori_loop(0, tokens // group - 1, lambda g, _: finish(g) or 0, 0)
        finish(jnp.int32(tokens // group - 1))

    plan_ref[small] = jnp.int32(span == QB // group)
    for r in range(GROUP - 1):
        line = iota((room * QB, tokens), 0) + plan_ref[sent + r] * QB
        chosen = (line == iota((room * QB, tokens), 1)).astype(f32).astype(bf16)
        pick_ref[r * room * QB : (r + 1) * room * QB, :] = chosen
    run(False)

    @pl.when(jnp.max(bad[...]) > 0)
    def _():
        run(True)

    attended = jnp.concatenate(
        [rows[pl.ds(h, tokens, stride=heads), :].astype(bf16) for h in range(heads)], axis=1
    )
    weight_copy.wait()
    width = out_refs[0].shape[1]
    step = 2 * LANES
    for k, out_ref in enumerate(out_refs):
        begin = 0 if outputs == 1 else jnp.where(here == k, width, 0)
        for n in range(0, width, step):
            some = wbuf[:, pl.ds(pl.multiple_of(begin + n, step), step)]
            out_ref[:, n : n + step] = jnp.dot(attended, some, preferred_element_type=f32)


VMEM = pl.BlockSpec(memory_space=pltpu.VMEM)
HBM = pl.BlockSpec(memory_space=pltpu.HBM)
SMEM = pl.BlockSpec(memory_space=pltpu.SMEM)


def own_layouts(queries, kv_rows):
    tokens, width = queries.shape
    heads = width // DH
    size = max(heads, PACK)
    f32, bf16 = jnp.float32, jnp.bfloat16
    return pl.pallas_call(
        own_kernel,
        out_shape=[
            jax.ShapeDtypeStruct((tokens * heads, DH), f32),
            jax.ShapeDtypeStruct((tokens, DH), bf16),
            jax.ShapeDtypeStruct((tokens // LANES, VR, LANES), bf16),
            jax.ShapeDtypeStruct((tokens * heads // size, size, DH), bf16),
            jax.ShapeDtypeStruct((tokens * heads // LANES, VR, LANES), f32),
        ],
        in_specs=[VMEM] * 2,
        out_specs=[VMEM] * 5,
        compiler_params=pltpu.CompilerParams(vmem_limit_bytes=16 * 2**20),
        cost_estimate=pl.CostEstimate(flops=10**9, bytes_accessed=4 * 2**20, transcendentals=0),
    )(queries, kv_rows)


def attended_and_projected(own, shards, table, weight, outputs):
    heads = own[0].shape[0] // own[1].shape[0]
    tokens = own[1].shape[0]
    sends = (GROUP - 1) * (tokens // QB // 2) * QB
    size = max(heads, PACK)
    f32, bf16 = jnp.float32, jnp.bfloat16
    return pl.pallas_call(
        functools.partial(attention_kernel, len(shards), outputs),
        out_shape=[jax.ShapeDtypeStruct((tokens, weight.shape[1] // outputs), f32)] * outputs
        + [
            jax.ShapeDtypeStruct((plan_places(tokens // QB)[-1],), jnp.int32),
            jax.ShapeDtypeStruct((sends, tokens), bf16),
        ],
        in_specs=[SMEM] + [VMEM] * 5 + [HBM] + [VMEM] * len(shards),
        out_specs=[VMEM] * outputs + [SMEM, VMEM],
        scratch_shapes=[
            pltpu.VMEM((W1, 4 * DH), bf16),
            pltpu.VMEM(weight.shape, bf16),
            pltpu.SemaphoreType.DMA,
            pltpu.VMEM((tokens, DH), bf16),
            pltpu.VMEM((W1, DH), bf16),
            pltpu.VMEM((W1 // LANES, VR, LANES), bf16),
            pltpu.VMEM((tokens // LANES, VR, LANES), bf16),
            pltpu.VMEM(((tokens + W2) * heads // size, size, DH), bf16),
            pltpu.VMEM(((tokens + W2) * heads // LANES, VR, LANES), f32),
            pltpu.VMEM((LANES, DH), bf16),
            pltpu.VMEM((VR, LANES), bf16),
            pltpu.VMEM((tokens, VR, LANES), f32),
            pltpu.VMEM((tokens, 8, LANES), f32),
            pltpu.VMEM((8, LANES), f32),
            pltpu.VMEM((tokens * heads, DH), f32),
        ],
        compiler_params=pltpu.CompilerParams(vmem_limit_bytes=43 * 2**20),
    )(table, *own, weight, *shards)

def shifted(block, axis, distance):
    devices = range(lax.axis_size(axis))
    return lax.ppermute(block, axis, [(i - distance, i) for i in devices if i - distance in devices])


def swapped(block, axis, bits):
    return lax.ppermute(block, axis, [(i, i ^ bits) for i in range(lax.axis_size(axis))])


def collect_window(kv_rows, back, own):
    if lax.axis_size("head") != 2 or back != 4:
        return [shifted(kv_rows, "ctx", back - k) for k in range(back)], own

    def taken(distances):
        devices = range(lax.axis_size("ctx"))
        route = [
            ((i - d) % len(devices) * 2 + h, i * 2 + h) for i in devices for h, d in enumerate(distances)
        ]
        return lax.ppermute(kv_rows, ("ctx", "head"), route)

    parts, own = lax.optimization_barrier(([taken((2, 4)), taken((1, 3))], own))
    held = jnp.concatenate(parts, axis=0)
    return [held, swapped(held, "head", 1)], own


def exchanged(terms, plan, position, blocks):
    room = blocks // 2
    pick, some_slots, whole_slots, few = plan

    def added(terms):
        return sum(terms[1:], terms[0]).astype(jnp.bfloat16)

    def placed(pieces, slots):
        tokens = blocks * QB
        rows = (slots[:, None] * QB + np.arange(QB, dtype=np.int32)[None, :]).reshape(-1)
        stored = position * tokens + jnp.arange(tokens, dtype=jnp.int32)
        pick = (rows[:, None] == stored[None, :]).astype(jnp.bfloat16)
        return lax.dot_general(
            jnp.concatenate(pieces, axis=0),
            pick,
            (((0,), (0,)), ((), ())),
            preferred_element_type=jnp.float32,
        ).astype(jnp.bfloat16)

    def some(*terms):
        own = added(terms)
        rows = jnp.dot(pick, own, preferred_element_type=jnp.float32).astype(jnp.bfloat16)
        rows = rows.reshape(GROUP - 1, room * QB, -1)
        pieces = [own] + [swapped(rows[r - 1], "ctx", r) for r in range(1, GROUP)]
        return placed(pieces, some_slots)

    def whole(*terms):
        own = added(terms)
        pieces = [own] + [swapped(own, "ctx", r) for r in range(1, GROUP)]
        return placed(pieces, whole_slots)

    return lax.cond(few, some, whole, *terms)


def body(queries, kv_rows, doc_start, destination, out_weight):
    position = lax.axis_index("ctx").astype(jnp.int32)
    tokens = queries.shape[0]
    blocks = tokens // QB
    here = lax.axis_index("head").astype(jnp.int32)
    table = jnp.concatenate([jnp.stack([position, here]), doc_start, destination])
    own = own_layouts(queries, kv_rows)
    shards, own = collect_window(kv_rows, W1 // tokens, own)
    outputs = 2 if len(shards) == 2 else 1
    results = attended_and_projected(own, shards, table, out_weight, outputs)
    partials, plan, pick = results[:outputs], results[outputs], results[outputs + 1]
    some, whole, small = plan_places(blocks)[-4:-1]
    parts = (pick, plan[some:whole], plan[whole:small], plan[small] > 0)
    if outputs == 2:
        terms = [partials[1], swapped(partials[0], "head", 1)]
    else:
        terms = [lax.psum_scatter(partials[0], "head", scatter_dimension=1, tiled=True)]
    return exchanged(terms, parts, position, blocks)


def solution(mesh):
    in_specs = (P("ctx", "head"), P("ctx", None), P(), P(), P("head", None))
    return jax.shard_map(
        body, mesh=mesh, in_specs=in_specs, out_specs=P("head", "ctx"), check_vma=False
    )
```

profile of v0, /device:TPU:28, one launch (start us, length us, event | category | flops | bytes accessed | tf_op | source)
XLA Modules:
  0.0 174.5 jit_solution(5704234772591600388)
XLA Ops:
  0.0 1.7 collective-permute-start.7
  1.7 1.0 copy-done
  2.7 0.9 copy-done.1
  3.6 1.0 shard_map.73
  4.6 0.8 collective-permute-done.6
  5.5 2.1 %collective-permute-done.7 = bf16[128,512]{1,0:T(8,128)(2,1)S(1)} collective-permute-done((bf16[128,512]{1,0:T(8,128)(2,1)}, bf16[128,512]{1,0:T(8,128)(2,1)S(1)}, u32[]{:S(2)}, u32[]{:S(2)}) %collective-permute-start.7) | collective-permute-done | bytes 131104 | tf_op jit(solution)/shard_map/ppermute | solution.py:463
  7.6 0.4 collective-permute-start.8
  8.0 0.1 pad_add_fusion.table_ref
  8.1 1.1 collective-permute-done.8.refs_1_
  9.2 35.4 %shard_map.74 = (f32[128,1024]{1,0:T(8,128)S(1)}, f32[128,1024]{1,0:T(8,128)S(1)}, s32[39]{0:T(128)S(1)}, bf16[192,128]{1,0:T(8,128)(2,1)S(1)}) custom-call(s32[130]{0:T(256)S(1)} %pad_add_fusion.table_ref, f32[2048,128]{1,0:T(8,128)S(1)} %get-tuple-element.66.q3, bf16[128,128]{1,0:T(8,128)(2,1)S(1)} %get-tuple-element.67.k1o, ...), custom_call_target="tpu_custom_call" | custom-call | tf_op jit(solution)/shard_map/pallas_call | solution.py:416
  44.6 0.4 collective-permute-start.9
  45.0 0.6 slice.23
  46.3 0.3 collective-permute-done.9
  46.6 127.2 %conditional.2 = (bf16[1024,128]{1,0:T(8,128)(2,1)S(1)}) conditional(s32[]{:T(128)} %bitcast.5, (f32[128,1024]{1,0:T(8,128)S(1)}, f32[128,1024]{1,0:T(8,128)S(1)}, s32[39]{0:T(128)S(1)}, s32[1,32]{1,0:T(1,128)S(1)}, s32[]{:T(128)}) %tuple.22, (f32[128,1024]{1,0:T(8,128)S(1)}, f32[128,1024]{1,0:T(8,128)S(1)}, bf16[192,128]{1,0:T(8,128)(2,1)S(1)}, ...), branch_computations={%region_0.0_spmd, %region_1.0_spmd} | conditional | flops 138740368 | bytes 5776848
  46.6 1.6 collective-permute-start.2
  48.3 111.5 %collective-permute-start.1 = (bf16[128,1024]{1,0:T(8,128)(2,1)S(1)}, bf16[128,1024]{1,0:T(8,128)(2,1)S(1)}, u32[]{:S(2)}, u32[]{:S(2)}) collective-permute-start(bf16[128,1024]{1,0:T(8,128)(2,1)S(1)} %add_convert_fusion), channel_id=1, source_target_pairs={{0,4},{2,6},{4,0},{6,2},{8,12},{10,14},{12,8},{14,10},{16,20},{18,... | collective-permute-start | bytes 786440 | tf_op jit(solution)/shard_map/cond/branch_0_fun/ppermute | solution.py:451
  159.8 1.4 collective-permute-start
  161.2 0.1 slice_multiply_fusion
  161.3 0.1 broadcast_add_fusion
  161.3 0.1 add.59
  161.4 9.9 %collective-permute-done.1 = bf16[128,1024]{1,0:T(8,128)(2,1)S(1)} collective-permute-done((bf16[128,1024]{1,0:T(8,128)(2,1)S(1)}, bf16[128,1024]{1,0:T(8,128)(2,1)S(1)}, u32[]{:S(2)}, u32[]{:S(2)}) %collective-permute-start.1) | collective-permute-done | bytes 262176 | tf_op jit(solution)/shard_map/cond/branch_0_fun/ppermute | solution.py:451
  171.3 1.9 %collective-permute-done = bf16[128,1024]{1,0:T(8,128)(2,1)S(1)} collective-permute-done((bf16[128,1024]{1,0:T(8,128)(2,1)S(1)}, bf16[128,1024]{1,0:T(8,128)(2,1)S(1)}, u32[]{:S(2)}, u32[]{:S(2)}) %collective-permute-start) | collective-permute-done | bytes 262176 | tf_op jit(solution)/shard_map/cond/branch_0_fun/ppermute | solution.py:451
  173.2 0.6 fusion
  173.8 0.7 copy-done.5
  (15 shorter events, 0.1 us)
Async XLA Ops:
  0.0 5.5 %collective-permute-start.6 = (bf16[128,512]{1,0:T(8,128)(2,1)}, bf16[128,512]{1,0:T(8,128)(2,1)S(1)}, u32[]{:S(2)}, u32[]{:S(2)}) collective-permute-start(bf16[128,512]{1,0:T(8,128)(2,1)} %kv_ref.1), channel_id=1, source_target_pairs={{28,0},{25,1},{30,2},{27,3},{0,4},{29,5},{2,6},{31,7},{4,8},{1,9},... | collective-permute-start | bytes 393224 | tf_op jit(solution)/shard_map/ppermute | solution.py:463
  0.0 7.5 %collective-permute-start.7 = (bf16[128,512]{1,0:T(8,128)(2,1)}, bf16[128,512]{1,0:T(8,128)(2,1)S(1)}, u32[]{:S(2)}, u32[]{:S(2)}) collective-permute-start(bf16[128,512]{1,0:T(8,128)(2,1)} %kv_ref.1), channel_id=1, source_target_pairs={{30,0},{27,1},{0,2},{29,3},{2,4},{31,5},{4,6},{1,7},{6,8},{3,9},{8... | collective-permute-start | bytes 393224 | tf_op jit(solution)/shard_map/ppermute | solution.py:463
  1.7 1.0 copy-start
  2.7 0.9 copy-start.1
  3.6 4.4 %copy-start.3 = (s32[64]{0:T(128)S(1)}, s32[64]{0:T(128)}, u32[]{:S(2)}) copy-start(s32[64]{0:T(128)} %param.12) | copy-start | bytes 772
  3.6 4.4 %copy-start.4 = (s32[64]{0:T(128)S(1)}, s32[64]{0:T(128)}, u32[]{:S(2)}) copy-start(s32[64]{0:T(128)} %param.11) | copy-start | bytes 772
  7.6 1.6 collective-permute-start.8
  8.1 38.5 %copy-start.2 = (s32[1,32]{1,0:T(1,128)S(1)}, s32[1,32]{1,0:T(1,128)}, u32[]{:S(2)}) copy-start(s32[1,32]{1,0:T(1,128)} %constant.21.clone) | copy-start | bytes 388
  44.6 2.0 %collective-permute-start.9 = (f32[128,1024]{1,0:T(8,128)S(1)}, f32[128,1024]{1,0:T(8,128)S(1)}, u32[]{:S(2)}, u32[]{:S(2)}) collective-permute-start(f32[128,1024]{1,0:T(8,128)S(1)} %get-tuple-element.75), channel_id=1, source_target_pairs={{0,1},{1,0},{2,3},{3,2},{4,5},{5,4},{6,7},{7,6},{8,9},{9,8},{10,11... | collective-permute-start | bytes 1572872 | tf_op jit(solution)/shard_map/ppermute | solution.py:451
  46.6 114.8 %collective-permute-start.2 = (bf16[128,1024]{1,0:T(8,128)(2,1)S(1)}, bf16[128,1024]{1,0:T(8,128)(2,1)S(1)}, u32[]{:S(2)}, u32[]{:S(2)}) collective-permute-start(bf16[128,1024]{1,0:T(8,128)(2,1)S(1)} %add_convert_fusion), channel_id=1, source_target_pairs={{0,6},{2,4},{4,2},{6,0},{8,14},{10,12},{12,10},{14,8},{16,22},{18,... | collective-permute-start | bytes 786440 | tf_op jit(solution)/shard_map/cond/branch_0_fun/ppermute | solution.py:451
  48.3 123.0 %collective-permute-start.1 = (bf16[128,1024]{1,0:T(8,128)(2,1)S(1)}, bf16[128,1024]{1,0:T(8,128)(2,1)S(1)}, u32[]{:S(2)}, u32[]{:S(2)}) collective-permute-start(bf16[128,1024]{1,0:T(8,128)(2,1)S(1)} %add_convert_fusion), channel_id=1, source_target_pairs={{0,4},{2,6},{4,0},{6,2},{8,12},{10,14},{12,8},{14,10},{16,20},{18,... | collective-permute-start | bytes 786440 | tf_op jit(solution)/shard_map/cond/branch_0_fun/ppermute | solution.py:451
  159.8 13.4 %collective-permute-start = (bf16[128,1024]{1,0:T(8,128)(2,1)S(1)}, bf16[128,1024]{1,0:T(8,128)(2,1)S(1)}, u32[]{:S(2)}, u32[]{:S(2)}) collective-permute-start(bf16[128,1024]{1,0:T(8,128)(2,1)S(1)} %add_convert_fusion), channel_id=1, source_target_pairs={{0,2},{2,0},{4,6},{6,4},{8,10},{10,8},{12,14},{14,12},{16,18},{18,... | collective-permute-start | bytes 786440 | tf_op jit(solution)/shard_map/cond/branch_0_fun/ppermute | solution.py:451
  173.8 0.7 copy-start.5
where the time goes:
time: 174 us
  starting transfers between devices  117 us (67%)
  Pallas kernels  36.4 us (21%)
  waiting for transfers between devices  16.1 us (9%)
  local copies, waits for them, and re-layouts  3.33 us (2%)
    ppermute x5, starting transfers between devices, swapped(): lax.ppermute(block, axis, [(i, i ^ bits) for i in range(lax.axis_size(axi...  115 us
    pallas_call x1, Pallas kernels, attended_and_projected(): pl.pallas_call(functools.partial(attention_kernel, len(shards), outputs),...  35.4 us
    ppermute x5, waiting for transfers between devices, swapped(): lax.ppermute(block, axis, [(i, i ^ bits) for i in range(lax.axis_size(axi...  13.1 us
  transfers between devices with their start and end apart: 7, of which 6 were waited for; matrix products, arithmetic and copies ran while one was open for 1% of the time, Pallas kernels for 1%

commit v1 on v0

--- a/solution.py
+++ b/solution.py
@@ -373,7 +373,7 @@
     )
     weight_copy.wait()
     width = out_refs[0].shape[1]
-    step = 2 * LANES
+    step = 4 * LANES
     for k, out_ref in enumerate(out_refs):
         begin = 0 if outputs == 1 else jnp.where(here == k, width, 0)
         for n in range(0, width, step):

time: 174 us -> 172 us (0.989)
  the two profiles are of different devices: /device:TPU:28 before, /device:TPU:0 now
where the time goes in v1:
time: 172 us
  starting transfers between devices  115 us (67%)
  Pallas kernels  36.4 us (21%)
  waiting for transfers between devices  15.8 us (9%)
  local copies, waits for them, and re-layouts  3.36 us (2%)
    ppermute x5, starting transfers between devices, swapped(): lax.ppermute(block, axis, [(i, i ^ bits) for i in range(lax.axis_size(axi...  111 us
    pallas_call x1, Pallas kernels, attended_and_projected(): pl.pallas_call(functools.partial(attention_kernel, len(shards), outputs),...  35.4 us
    ppermute x5, waiting for transfers between devices, swapped(): lax.ppermute(block, axis, [(i, i ^ bits) for i in range(lax.axis_size(axi...  9.72 us
    ppermute x2, waiting for transfers between devices, taken(): return lax.ppermute(kv_rows, ('ctx', 'head'), route)  6.03 us
    ppermute x2, starting transfers between devices, taken(): return lax.ppermute(kv_rows, ('ctx', 'head'), route)  4.46 us
  transfers between devices with their start and end apart: 7, of which 6 were waited for; matrix products, arithmetic and copies ran while one was open for 1% of the time, Pallas kernels for 1%

profile of v1, /device:TPU:0, one launch (start us, length us, event | category | flops | bytes accessed | tf_op | source)
XLA Modules:
  0.0 172.4 jit_solution(15780228567016356850)
XLA Ops:
  0.0 3.0 %collective-permute-start.6 = (bf16[128,512]{1,0:T(8,128)(2,1)}, bf16[128,512]{1,0:T(8,128)(2,1)S(1)}, u32[]{:S(2)}, u32[]{:S(2)}) collective-permute-start(bf16[128,512]{1,0:T(8,128)(2,1)} %kv_ref.1), channel_id=1, source_target_pairs={{28,0},{25,1},{30,2},{27,3},{0,4},{29,5},{2,6},{31,7},{4,8},{1,9},... | collective-permute-start | bytes 393224 | tf_op jit(solution)/shard_map/ppermute | solution.py:463
  3.0 1.5 collective-permute-start.7
  4.5 1.0 copy-done
  5.5 0.9 copy-done.1
  6.4 1.0 shard_map.73
  7.4 3.0 %collective-permute-done.6 = bf16[128,512]{1,0:T(8,128)(2,1)S(1)} collective-permute-done((bf16[128,512]{1,0:T(8,128)(2,1)}, bf16[128,512]{1,0:T(8,128)(2,1)S(1)}, u32[]{:S(2)}, u32[]{:S(2)}) %collective-permute-start.6) | collective-permute-done | bytes 131104 | tf_op jit(solution)/shard_map/ppermute | solution.py:463
  10.4 3.1 %collective-permute-done.7 = bf16[128,512]{1,0:T(8,128)(2,1)S(1)} collective-permute-done((bf16[128,512]{1,0:T(8,128)(2,1)}, bf16[128,512]{1,0:T(8,128)(2,1)S(1)}, u32[]{:S(2)}, u32[]{:S(2)}) %collective-permute-start.7) | collective-permute-done | bytes 131104 | tf_op jit(solution)/shard_map/ppermute | solution.py:463
  13.5 0.1 collective-permute-start.8
  13.6 0.1 pad_add_fusion.table_ref
  13.7 1.4 collective-permute-done.8.refs_1_
  15.1 35.4 %shard_map.74 = (f32[128,1024]{1,0:T(8,128)S(1)}, f32[128,1024]{1,0:T(8,128)S(1)}, s32[39]{0:T(128)S(1)}, bf16[192,128]{1,0:T(8,128)(2,1)S(1)}) custom-call(s32[130]{0:T(256)S(1)} %pad_add_fusion.table_ref, f32[2048,128]{1,0:T(8,128)S(1)} %get-tuple-element.66.q3, bf16[128,128]{1,0:T(8,128)(2,1)S(1)} %get-tuple-element.67.k1o, ...), custom_call_target="tpu_custom_call" | custom-call | tf_op jit(solution)/shard_map/pallas_call | solution.py:416
  50.5 0.2 collective-permute-start.9
  50.7 0.6 slice.23
  51.9 0.5 collective-permute-done.9
  52.4 119.3 %conditional.2 = (bf16[1024,128]{1,0:T(8,128)(2,1)S(1)}) conditional(s32[]{:T(128)} %bitcast.5, (f32[128,1024]{1,0:T(8,128)S(1)}, f32[128,1024]{1,0:T(8,128)S(1)}, s32[39]{0:T(128)S(1)}, s32[1,32]{1,0:T(1,128)S(1)}, s32[]{:T(128)}) %tuple.22, (f32[128,1024]{1,0:T(8,128)S(1)}, f32[128,1024]{1,0:T(8,128)S(1)}, bf16[192,128]{1,0:T(8,128)(2,1)S(1)}, ...), branch_computations={%region_0.0_spmd, %region_1.0_spmd} | conditional | flops 138740368 | bytes 5776848
  52.5 0.2 fusion.12
  52.9 110.3 %collective-permute-start.5 = (bf16[64,1024]{1,0:T(8,128)(2,1)S(1)}, bf16[64,1024]{1,0:T(8,128)(2,1)S(1)}, u32[]{:S(2)}, u32[]{:S(2)}) collective-permute-start(bf16[64,1024]{1,0:T(8,128)(2,1)S(1)} %get-tuple-element.78), channel_id=1, source_target_pairs={{0,6},{2,4},{4,2},{6,0},{8,14},{10,12},{12,10},{14,8},{16,22},{18,... | collective-permute-start | bytes 393224 | tf_op jit(solution)/shard_map/cond/branch_1_fun/ppermute | solution.py:451
  163.2 0.1 slice_multiply_fusion.1
  163.3 0.1 broadcast_add_fusion.1
  163.4 0.1 add.67
  163.5 6.4 %collective-permute-done.5 = bf16[64,1024]{1,0:T(8,128)(2,1)S(1)} collective-permute-done((bf16[64,1024]{1,0:T(8,128)(2,1)S(1)}, bf16[64,1024]{1,0:T(8,128)(2,1)S(1)}, u32[]{:S(2)}, u32[]{:S(2)}) %collective-permute-start.5) | collective-permute-done | bytes 131104 | tf_op jit(solution)/shard_map/cond/branch_1_fun/ppermute | solution.py:451
  169.9 1.4 collective-permute-done.4
  171.2 0.5 fusion.13
  171.7 0.7 copy-done.5
  (17 shorter events, 0.2 us)
Async XLA Ops:
  0.0 10.4 %collective-permute-start.6 = (bf16[128,512]{1,0:T(8,128)(2,1)}, bf16[128,512]{1,0:T(8,128)(2,1)S(1)}, u32[]{:S(2)}, u32[]{:S(2)}) collective-permute-start(bf16[128,512]{1,0:T(8,128)(2,1)} %kv_ref.1), channel_id=1, source_target_pairs={{28,0},{25,1},{30,2},{27,3},{0,4},{29,5},{2,6},{31,7},{4,8},{1,9},... | collective-permute-start | bytes 393224 | tf_op jit(solution)/shard_map/ppermute | solution.py:463
  3.0 10.5 %collective-permute-start.7 = (bf16[128,512]{1,0:T(8,128)(2,1)}, bf16[128,512]{1,0:T(8,128)(2,1)S(1)}, u32[]{:S(2)}, u32[]{:S(2)}) collective-permute-start(bf16[128,512]{1,0:T(8,128)(2,1)} %kv_ref.1), channel_id=1, source_target_pairs={{30,0},{27,1},{0,2},{29,3},{2,4},{31,5},{4,6},{1,7},{6,8},{3,9},{8... | collective-permute-start | bytes 393224 | tf_op jit(solution)/shard_map/ppermute | solution.py:463
  4.5 1.0 copy-start
  5.5 0.9 copy-start.1
  6.4 7.2 %copy-start.3 = (s32[64]{0:T(128)S(1)}, s32[64]{0:T(128)}, u32[]{:S(2)}) copy-start(s32[64]{0:T(128)} %param.12) | copy-start | bytes 772
  6.4 7.2 %copy-start.4 = (s32[64]{0:T(128)S(1)}, s32[64]{0:T(128)}, u32[]{:S(2)}) copy-start(s32[64]{0:T(128)} %param.11) | copy-start | bytes 772
  13.5 1.6 collective-permute-start.8
  13.7 38.8 %copy-start.2 = (s32[1,32]{1,0:T(1,128)S(1)}, s32[1,32]{1,0:T(1,128)}, u32[]{:S(2)}) copy-start(s32[1,32]{1,0:T(1,128)} %constant.21.clone) | copy-start | bytes 388
  50.5 2.0 %collective-permute-start.9 = (f32[128,1024]{1,0:T(8,128)S(1)}, f32[128,1024]{1,0:T(8,128)S(1)}, u32[]{:S(2)}, u32[]{:S(2)}) collective-permute-start(f32[128,1024]{1,0:T(8,128)S(1)} %get-tuple-element.75), channel_id=1, source_target_pairs={{0,1},{1,0},{2,3},{3,2},{4,5},{5,4},{6,7},{7,6},{8,9},{9,8},{10,11... | collective-permute-start | bytes 1572872 | tf_op jit(solution)/shard_map/ppermute | solution.py:451
  52.8 110.7 %collective-permute-start.3 = (bf16[64,1024]{1,0:T(8,128)(2,1)S(1)}, bf16[64,1024]{1,0:T(8,128)(2,1)S(1)}, u32[]{:S(2)}, u32[]{:S(2)}) collective-permute-start(bf16[64,1024]{1,0:T(8,128)(2,1)S(1)} %get-tuple-element.77), channel_id=1, source_target_pairs={{0,2},{2,0},{4,6},{6,4},{8,10},{10,8},{12,14},{14,12},{16,18},{18,... | collective-permute-start | bytes 393224 | tf_op jit(solution)/shard_map/cond/branch_1_fun/ppermute | solution.py:451
  52.9 117.0 %collective-permute-start.5 = (bf16[64,1024]{1,0:T(8,128)(2,1)S(1)}, bf16[64,1024]{1,0:T(8,128)(2,1)S(1)}, u32[]{:S(2)}, u32[]{:S(2)}) collective-permute-start(bf16[64,1024]{1,0:T(8,128)(2,1)S(1)} %get-tuple-element.78), channel_id=1, source_target_pairs={{0,6},{2,4},{4,2},{6,0},{8,14},{10,12},{12,10},{14,8},{16,22},{18,... | collective-permute-start | bytes 393224 | tf_op jit(solution)/shard_map/cond/branch_1_fun/ppermute | solution.py:451
  163.2 8.0 %collective-permute-start.4 = (bf16[64,1024]{1,0:T(8,128)(2,1)S(1)}, bf16[64,1024]{1,0:T(8,128)(2,1)S(1)}, u32[]{:S(2)}, u32[]{:S(2)}) collective-permute-start(bf16[64,1024]{1,0:T(8,128)(2,1)S(1)} %get-tuple-element.79), channel_id=1, source_target_pairs={{0,4},{2,6},{4,0},{6,2},{8,12},{10,14},{12,8},{14,10},{16,20},{18,... | collective-permute-start | bytes 393224 | tf_op jit(solution)/shard_map/cond/branch_1_fun/ppermute | solution.py:451
  171.7 0.7 copy-start.5
